TPU v7x, 512 devices: a whole 4x4x16 slice. The times are simulated.
512 devices in a mesh: tm: 8 (over y, z_hi), space: 64 (over x, z_lo, core).
Axes of the slice: x: 4, y: 4, z: 16 (z_hi: 2, z_lo: 8; z = z_hi * 8 + z_lo), core: 2. Of those that a mesh axis runs over, the one named last changes fastest.
Arguments:
- forcing: float32 [32, 2, 64, 128, 128], P('tm', None, 'space'), may hold values from -6 to 6
- init_state: float32 [2, 64, 128, 128], P(None, 'space'), may hold values from -6 to 6
- prev_last: float32 [2, 64, 128, 128], P(None, 'space'), may hold values from -6 to 6
- diff_h: float32 [64, 128, 128], P('space'), may hold values from 0.04 to 0.24
- vel_x: float32 [64, 128, 128], P('space'), may hold values from -0.2 to 0.2
- vel_y: float32 [64, 128, 128], P('space'), may hold values from -0.2 to 0.2
- diff_z: float32 [64, 128, 128], P('space'), may hold values from 0.05 to 0.4
Outputs:
- iterate: float32 [32, 2, 64, 128, 128], P('tm', None, 'space')
All inputs are finite; a program needn't handle non-finite values.
Results may differ from a plain program's by a relative error of at most 0.0003.
Values sent between devices are 32-bit elements; how exact they have to be, the bound alone decides.
No kernel may reach another device: no remote copies, remote signals or barrier semaphores. Data moves between devices by JAX's collectives and lax.ppermute only.
A program may use at most 64 MiB of HBM per device.

v0:
```python
import math

import jax
import jax.numpy as jnp
from jax import lax
from jax.sharding import PartitionSpec as P

SWEEPS = 2


corner_weight = 0.5


def with_halo(cells, sides, width):
    for axis, dim in sides:
        count = lax.axis_size(axis)
        ends = count - 1
        head = lax.slice_in_dim(cells, 0, width, axis=dim)
        tail = lax.slice_in_dim(cells, cells.shape[dim] - width, cells.shape[dim], axis=dim)
        cells = jnp.concatenate(
            [
                lax.ppermute(tail, axis, [(i, (i + 1) % count) for i in range(ends)]),
                cells,
                lax.ppermute(head, axis, [((i + 1) % count, i) for i in range(ends)]),
            ],
            axis=dim,
        )
    return cells


def phase_table(rows, cols, total):
    product = rows[:, None] * cols[None, :] % total
    return product.astype(jnp.float32) * (2.0 * math.pi / total)


def along_y(field, diff_h, vel_y):
    pads = [(0, 0)] * (field.ndim - 2) + [(1, 1), (0, 0)]
    padded = jnp.pad(field, pads)
    return (
        field
        + (diff_h + vel_y) * padded[..., :-2, :]
        - 2.0 * diff_h * field
        + (diff_h - vel_y) * padded[..., 2:, :]
    )


def along_z(field, diff_z):
    pads = [(0, 0)] * (field.ndim - 1) + [(1, 1)]
    padded = jnp.pad(field, pads)
    return diff_z * (padded[..., :-2] - 2.0 * field + padded[..., 2:])


def along_x(center, left, right, diff_h, vel_x):
    return center + (diff_h + vel_x) * left - 2.0 * diff_h * center + (diff_h - vel_x) * right


def operate(stacked, diff_h, vel_x, vel_y, diff_z):
    smoothed = along_y(stacked, diff_h, vel_y)
    extended = with_halo(smoothed, (("space", 3),), 1)
    mixed = along_x(smoothed, extended[:, :, :, :-2], extended[:, :, :, 2:], diff_h, vel_x)
    return mixed - stacked + along_z(stacked, diff_z)


def relax(spec_re, spec_im, freq_f, total, coeffs, apply_op):
    diff_h, vel_x, vel_y, diff_z = coeffs
    ratio = jnp.exp(jnp.float32(math.log(corner_weight) / total))
    theta = freq_f * (2.0 * math.pi / total)
    lam_re = (1.0 - ratio * jnp.cos(theta))[:, None, None, None, None]
    lam_im = (ratio * jnp.sin(theta))[:, None, None, None, None]
    shift = 1.0 - (1.0 - 2.0 * diff_h) * (1.0 - 2.0 * diff_h) + 2.0 * diff_z
    real_d = lam_re + shift
    denom = real_d * real_d + lam_im * lam_im
    sol_re = (spec_re * real_d + spec_im * lam_im) / denom
    sol_im = (spec_im * real_d - spec_re * lam_im) / denom
    for sweep in range(SWEEPS):
        image = apply_op(jnp.stack([sol_re, sol_im]), diff_h, vel_x, vel_y, diff_z)
        apply_re = lam_re * sol_re - lam_im * sol_im - image[0]
        apply_im = lam_re * sol_im + lam_im * sol_re - image[1]
        resid_re = spec_re - apply_re
        resid_im = spec_im - apply_im
        sol_re = sol_re + (resid_re * real_d + resid_im * lam_im) / denom
        sol_im = sol_im + (resid_im * real_d - resid_re * lam_im) / denom
    return (sol_re, sol_im)


def shards(forcing, init_state, prev_last, diff_h, vel_x, vel_y, diff_z):
    steps_dev = forcing.shape[0]
    groups = lax.axis_size("tm")
    total = steps_dev * groups
    local_steps = lax.axis_index("tm") * steps_dev + jnp.arange(steps_dev, dtype=jnp.int32)
    local_f = local_steps.astype(jnp.float32)
    row_zero = (local_steps == 0).astype(jnp.float32)[:, None, None, None, None]
    rhs = forcing + row_zero * (init_state - corner_weight * prev_last)[None]
    power = jnp.exp(local_f * (math.log(corner_weight) / total))
    scaled = rhs * power[:, None, None, None, None]
    shape = forcing.shape
    coeffs = (diff_h, vel_x, vel_y, diff_z)
    empty = jnp.zeros(shape, jnp.float32)
    piece = lax.all_gather(scaled, "tm", axis=0, tiled=True)
    count = piece.shape[0]
    cols = jnp.arange(count, dtype=jnp.int32)
    angle = phase_table(local_steps, cols, total)
    flat = piece.reshape(count, -1)
    part_re = jnp.dot(jnp.cos(angle), flat, precision=lax.Precision.HIGHEST).reshape(shape)
    part_im = jnp.dot(jnp.sin(angle), flat, precision=lax.Precision.HIGHEST).reshape(shape)
    spec_im = (empty, empty)[1] - part_im
    sol_re, sol_im = relax(part_re, spec_im, local_f, total, coeffs, operate)
    pieces = (
        lax.all_gather(sol_re, "tm", axis=0, tiled=True),
        lax.all_gather(sol_im, "tm", axis=0, tiled=True),
    )
    count = pieces[0].shape[0]
    cols = jnp.arange(count, dtype=jnp.int32)
    angle = phase_table(local_steps, cols, total)
    first = jnp.dot(jnp.cos(angle), pieces[0].reshape(count, -1), precision=lax.Precision.HIGHEST)
    second = jnp.dot(jnp.sin(angle), pieces[1].reshape(count, -1), precision=lax.Precision.HIGHEST)
    summed = (first - second).reshape(shape)
    back = jnp.exp(local_f * (-math.log(corner_weight) / total)) / total
    return summed * back[:, None, None, None, None]


def solution(mesh):
    return jax.shard_map(
        shards,
        mesh=mesh,
        in_specs=(
            P("tm", None, "space", None, None),
            P(None, "space", None, None),
            P(None, "space", None, None),
            P("space", None, None),
            P("space", None, None),
            P("space", None, None),
            P("space", None, None),
        ),
        out_specs=P("tm", None, "space", None, None),
        check_vma=False,
    )
```

profile of v0, /device:TPU:1, one launch (start us, length us, event | category | flops | bytes accessed | tf_op | source)
XLA Modules:
  0.0 635.7 jit_solution(7037856041600275865)
XLA Ops:
  6.5 1.0 subtract_bitcast_fusion
  7.5 2.0 add_multiply_fusion
  9.7 1.0 add_bitcast_fusion
  10.8 183.8 %all-gather.6.cloned.1.call-done = f32[32,2,1,128,128]{4,3,2,1,0:T(8,128)} async-done(((f32[4,2,1,128,128]{4,3,2,1,0:T(8,128)}), f32[32,2,1,128,128]{4,3,2,1,0:T(8,128)}) %all-gather.6.cloned.1.call-update) | async-done | bytes 4194320 | tf_op jit(solution)/shard_map/all_gather | solution.py:99
  194.6 4.6 copy.43
  199.2 0.7 copy.22
  200.0 4.4 fusion.12
  204.4 4.6 fusion.7
  209.0 0.4 fusion.59
  209.4 0.2 pad_maximum_fusion
  209.6 0.4 multiply_add_fusion.1
  210.0 3.0 collective-permute-start.1
  213.0 2.6 collective-permute-start
  215.6 21.8 %collective-permute-done.1 = f32[2,4,2,1,128,128]{5,1,4,2,3,0:T(4,128)S(1)} collective-permute-done((f32[2,4,2,1,128,128]{5,1,4,2,3,0:T(4,128)S(1)}, f32[2,4,2,1,128,128]{5,1,4,2,3,0:T(4,128)S(1)}, u32[]{:S(2)}, u32[]{:S(2)}) %collective-permute-start.1) | collective-permute-done | bytes 1048608 | tf_op jit(solution)/shard_map/ppermute | solution.py:24
  237.4 1.7 fusion.18
  239.1 1.0 divide_add_fusion.2
  240.1 0.2 pad_maximum_fusion.1
  240.4 0.4 multiply_add_fusion
  240.8 1.9 collective-permute-start.3
  242.7 3.6 collective-permute-start.2
  246.4 10.5 %collective-permute-done.3 = f32[2,4,2,1,128,128]{5,1,4,2,3,0:T(4,128)S(1)} collective-permute-done((f32[2,4,2,1,128,128]{5,1,4,2,3,0:T(4,128)S(1)}, f32[2,4,2,1,128,128]{5,1,4,2,3,0:T(4,128)S(1)}, u32[]{:S(2)}, u32[]{:S(2)}) %collective-permute-start.3) | collective-permute-done | bytes 1048608 | tf_op jit(solution)/shard_map/ppermute | solution.py:24
  256.9 1.2 collective-permute-done.2
  258.1 1.7 fusion.22
  259.8 0.8 divide_add_fusion
  260.6 0.8 copy.16
  261.4 0.3 all-gather.10.cloned.1.call-start
  261.7 0.9 copy.17
  262.6 186.4 %all-gather.8.cloned.1.call-done = f32[32,2,128,128]{3,2,1,0:T(8,128)} async-done(((f32[4,2,128,128]{3,2,1,0:T(8,128)}), f32[32,2,128,128]{3,2,1,0:T(8,128)}) %all-gather.8.cloned.1.call-update) | async-done | bytes 4194320 | tf_op jit(solution)/shard_map/all_gather | solution.py:109
  449.0 6.5 %fusion.2 = f32[4,32768]{1,0:T(4,128)S(1)} fusion(f32[4,8,256,128]{3,2,1,0:T(8,128)} %bitcast.107, s32[4]{0:T(128)S(1)} %iota_add_fusion), kind=kOutput, calls=%fused_computation.3 | convolution fusion | flops 50333440 | bytes 4718608 | tf_op jit(solution)/shard_map/dot_general | solution.py:115
  455.5 166.3 %all-gather.10.cloned.1.call-done = f32[32,2,128,128]{3,2,1,0:T(8,128)} async-done(((f32[4,2,128,128]{3,2,1,0:T(8,128)}), f32[32,2,128,128]{3,2,1,0:T(8,128)}) %all-gather.10.cloned.1.call-update) | async-done | bytes 4194320 | tf_op jit(solution)/shard_map/all_gather | solution.py:110
  621.7 6.5 %fusion.9 = f32[1,4,256,128]{3,1,2,0:T(4,128)S(1)} fusion(f32[4,32768]{1,0:T(4,128)S(1)} %fusion.2, f32[4,8,256,128]{3,2,1,0:T(8,128)} %bitcast.109, s32[4]{0:T(128)S(1)} %iota_add_fusion), kind=kOutput, calls=%fused_computation.15 | convolution fusion | flops 50464512 | bytes 5242896 | tf_op jit(solution)/shard_map/dot_general | solution.py:116
  628.3 0.9 bitcast_multiply_fusion
  (15 shorter events, 0.4 us)
Async XLA Ops:
  6.5 188.1 %all-gather.6.cloned.1.call-start = ((), (), s32[]{:S(2)}) async-start(), calls=%async_computation | async-start | bytes 4718592 | tf_op jit(solution)/shard_map/all_gather | solution.py:99
  9.5 439.5 %all-gather.8.cloned.1.call-start = ((), (), s32[]{:S(2)}) async-start(), calls=%async_computation.1 | async-start | bytes 4718592 | tf_op jit(solution)/shard_map/all_gather | solution.py:109
  209.0 28.4 %copy-start = (f32[1,128,128]{2,1,0:T(8,128)S(1)}, f32[1,128,128]{2,1,0:T(8,128)}, u32[]{:S(2)}) copy-start(f32[1,128,128]{2,1,0:T(8,128)} %param.13) | copy-start | bytes 196612
  210.0 27.4 %collective-permute-start.1 = (f32[2,4,2,1,128,128]{5,1,4,2,3,0:T(4,128)S(1)}, f32[2,4,2,1,128,128]{5,1,4,2,3,0:T(4,128)S(1)}, u32[]{:S(2)}, u32[]{:S(2)}) collective-permute-start(f32[2,4,2,1,128,128]{5,1,4,2,3,0:T(4,128)S(1)} %multiply_add_fusion.1), channel_id=1, source_target_pairs={{1,0},{2,1},{3,2},{4,3},{5,4},{6,5},{7,6},{8,7},{9,8},{10,9},{11,1... | collective-permute-start | bytes 3145736 | tf_op jit(solution)/shard_map/ppermute | solution.py:24
  213.0 24.4 %collective-permute-start = (f32[2,4,2,1,128,128]{5,1,4,2,3,0:T(4,128)S(1)}, f32[2,4,2,1,128,128]{5,1,4,2,3,0:T(4,128)S(1)}, u32[]{:S(2)}, u32[]{:S(2)}) collective-permute-start(f32[2,4,2,1,128,128]{5,1,4,2,3,0:T(4,128)S(1)} %multiply_add_fusion.1), channel_id=1, source_target_pairs={{0,1},{1,2},{2,3},{3,4},{4,5},{5,6},{6,7},{7,8},{8,9},{9,10},{10,1... | collective-permute-start | bytes 3145736 | tf_op jit(solution)/shard_map/ppermute | solution.py:22
  240.8 16.1 %collective-permute-start.3 = (f32[2,4,2,1,128,128]{5,1,4,2,3,0:T(4,128)S(1)}, f32[2,4,2,1,128,128]{5,1,4,2,3,0:T(4,128)S(1)}, u32[]{:S(2)}, u32[]{:S(2)}) collective-permute-start(f32[2,4,2,1,128,128]{5,1,4,2,3,0:T(4,128)S(1)} %multiply_add_fusion), channel_id=1, source_target_pairs={{1,0},{2,1},{3,2},{4,3},{5,4},{6,5},{7,6},{8,7},{9,8},{10,9},{11,1... | collective-permute-start | bytes 3145736 | tf_op jit(solution)/shard_map/ppermute | solution.py:24
  242.7 15.4 %collective-permute-start.2 = (f32[2,4,2,1,128,128]{5,1,4,2,3,0:T(4,128)S(1)}, f32[2,4,2,1,128,128]{5,1,4,2,3,0:T(4,128)S(1)}, u32[]{:S(2)}, u32[]{:S(2)}) collective-permute-start(f32[2,4,2,1,128,128]{5,1,4,2,3,0:T(4,128)S(1)} %multiply_add_fusion), channel_id=1, source_target_pairs={{0,1},{1,2},{2,3},{3,4},{4,5},{5,6},{6,7},{7,8},{8,9},{9,10},{10,1... | collective-permute-start | bytes 3145736 | tf_op jit(solution)/shard_map/ppermute | solution.py:22
  261.4 360.3 %all-gather.10.cloned.1.call-start = ((), (), s32[]{:S(2)}) async-start(), calls=%async_computation.2 | async-start | bytes 4718592 | tf_op jit(solution)/shard_map/all_gather | solution.py:110
Sparse Core Ops, SparseCore 0:
  10.6 183.9 all-gather.5
  261.6 187.4 all-gather.7
  452.2 169.4 all-gather.9
where the time goes:
time: 636 us
  waiting for transfers between devices  570 us (90%)
  matrix products  21.9 us (3%)
  between operations  13.3 us (2%)
  other arithmetic  12 us (2%)
  starting transfers between devices  11.4 us (2%)
  local copies, waits for them, and re-layouts  7.12 us (1%)
    all_gather x1, waiting for transfers between devices, shards(): lax.all_gather(sol_re, 'tm', axis=0, tiled=True)  186 us
    all_gather x1, waiting for transfers between devices, shards(): piece = lax.all_gather(scaled, 'tm', axis=0, tiled=True)  184 us
    all_gather x1, waiting for transfers between devices, shards(): lax.all_gather(sol_im, 'tm', axis=0, tiled=True)  166 us
    ppermute x2, waiting for transfers between devices, with_halo(): lax.ppermute(head, axis, [((i + 1) % count, i) for i in range(ends)])  32.3 us
  transfers between devices with their start and end apart: 7, of which 6 were waited for; matrix products, arithmetic and copies ran while one was open for 1% of the time, Pallas kernels for 0%

commit v1 on v0

v1 whole, which is shorter than its diff:
```python
import math

import jax
import jax.numpy as jnp
from jax import lax
from jax.experimental import pallas as pl
from jax.experimental.pallas import tpu as pltpu
from jax.sharding import PartitionSpec as P

CORNER = 0.5
NT = 32
LOG_G = math.log(CORNER) / NT
G = math.exp(LOG_G)
ROWS = 32
WIDE = ROWS + 4
SMOOTH = ROWS + 2
VMEM = 24 * 1024 * 1024

CHIPS_X, CHIPS_Y, CHIPS_Z, CORES = 4, 4, 16, 2


def flat_index(x, y, z, core):
    half = CHIPS_Z // 2
    return (y * 2 + z // half) * (CHIPS_X * half * CORES) + (x * half + z % half) * CORES + core


def x_neighbours():
    pairs = []
    half = CHIPS_Z // 2
    for x in range(CHIPS_X):
        for y in range(CHIPS_Y):
            for z in range(CHIPS_Z):
                here = flat_index(x, y, z, 0)
                pairs.append((here, flat_index(x, y, z, 1)))
                step = x + 1 if z % half == half - 1 else x
                if step < CHIPS_X:
                    pairs.append((flat_index(x, y, z, 1), flat_index(step, y, (z + 1) % CHIPS_Z, 0)))
    return pairs


def real_fft(values):
    n = len(values)
    if n == 1:
        return [(values[0], None)]
    if n == 2:
        return [(values[0] + values[1], None), (values[0] - values[1], None)]
    even, odd = real_fft(values[0::2]), real_fft(values[1::2])
    out = [None] * (n // 2 + 1)
    out[0] = (even[0][0] + odd[0][0], None)
    out[n // 2] = (even[0][0] - odd[0][0], None)
    for k in range(1, n // 4):
        c, s = math.cos(2 * math.pi * k / n), math.sin(2 * math.pi * k / n)
        er, ei = even[k]
        orr, oi = odd[k]
        tr = c * orr + s * oi
        ti = c * oi - s * orr
        out[k] = (er + tr, ei + ti)
        out[n // 2 - k] = (er - tr, ti - ei)
    out[n // 4] = (even[n // 4][0], -odd[n // 4][0])
    return out


def real_ifft(spec):
    n = 2 * (len(spec) - 1)
    if n == 2:
        return [spec[0][0] + spec[1][0], spec[0][0] - spec[1][0]]
    even, odd = [None] * (n // 4 + 1), [None] * (n // 4 + 1)
    even[0] = (spec[0][0] + spec[n // 2][0], None)
    odd[0] = (spec[0][0] - spec[n // 2][0], None)
    for k in range(1, n // 4):
        c, s = math.cos(2 * math.pi * k / n), math.sin(2 * math.pi * k / n)
        ar, ai = spec[k]
        br, bi = spec[n // 2 - k]
        even[k] = (ar + br, ai - bi)
        dr, di = ar - br, ai + bi
        odd[k] = (c * dr - s * di, c * di + s * dr)
    even[n // 4] = (2.0 * spec[n // 4][0], None)
    odd[n // 4] = (-2.0 * spec[n // 4][1], None)
    first, second = real_ifft(even), real_ifft(odd)
    out = [None] * n
    out[0::2], out[1::2] = first, second
    return out


def inverses(pair, h):
    if pair == 0:
        return 1.0 / (h + (1.0 - G)), 1.0 / (h + (1.0 + G))
    theta = 2.0 * math.pi * pair / NT
    real = h + (1.0 - G * math.cos(theta))
    imag = G * math.sin(theta)
    scale = 1.0 / (real * real + imag * imag)
    return real * scale, imag * scale


def apply_inverse(pair, inv, first, second):
    if pair == 0:
        return first * inv[0], second * inv[1]
    return first * inv[0] + second * inv[1], second * inv[0] - first * inv[1]


def pack_kernel(ids, forcing, init, prev, diff_h, vel_x, vel_y, diff_z, blocks, coeffs):
    quarter, odd_x = ids[0], ids[1]
    first = (ids[2] == 0).astype(jnp.float32)
    for half in range(2):
        tracer = odd_x if half == 0 else 1 - odd_x
        for part in range(4):
            dest = 2 * part + half
            low, high = max(ROWS * part - 2, 0), min(ROWS * part + ROWS + 2, 128)
            skip = low - (ROWS * part - 2)
            for step in range(4):
                value = forcing[step, tracer, low:high, :]
                if step == 0:
                    value = value + first * (init[tracer, low:high, :] - CORNER * prev[tracer, low:high, :])
                base = WIDE * step
                blocks[dest, base + skip : base + skip + high - low, :] = value
                if skip:
                    blocks[dest, base : base + skip, :] = jnp.zeros((skip, 128), jnp.float32)
                rest = WIDE - skip - (high - low)
                if rest:
                    blocks[dest, base + WIDE - rest : base + WIDE, :] = jnp.zeros((rest, 128), jnp.float32)
    for part in range(4):

        @pl.when(quarter == part)
        def _():
            low, high = max(ROWS * part - 2, 0), min(ROWS * part + ROWS + 2, 128)
            skip = low - (ROWS * part - 2)
            if part in (0, 3):
                coeffs[...] = jnp.zeros(coeffs.shape, jnp.float32)
            for i, ref in enumerate((diff_h, vel_x, vel_y, diff_z)):
                coeffs[i, skip : skip + high - low, :] = ref[low:high, :]


def chunks(start, count):
    out = list(range(start, start + count - 7, 8))
    if count % 8:
        out.append(start + count - 8)
    return out


def smooth_rows(coeffs, field, start, index):
    d = coeffs[0, start : start + 8, :]
    vy = coeffs[2, start : start + 8, :]
    return (
        (1.0 - 2.0 * d) * field[index, start : start + 8, :]
        + (d + vy) * field[index, start - 1 : start + 7, :]
        + (d - vy) * field[index, start + 1 : start + 9, :]
    )


def shift_of(d, dz):
    a = 1.0 - 2.0 * d
    return 1.0 - a * a + 2.0 * dz


def first_kernel(gathered, coeffs, start_field, smoothed):
    for r in chunks(0, WIDE):
        values = []
        for n in range(NT):
            base = WIDE * (n % 4) + r
            value = gathered[n // 4, base : base + 8, :]
            values.append(value * math.exp(n * LOG_G) if n else value)
        spec = real_fft(values)
        h = shift_of(coeffs[0, r : r + 8, :], coeffs[3, r : r + 8, :])
        for pair in range(16):
            a, b = (spec[0][0], spec[16][0]) if pair == 0 else spec[pair]
            ya, yb = apply_inverse(pair, inverses(pair, h), a, b)
            start_field[2 * pair, r : r + 8, :] = ya
            start_field[2 * pair + 1, r : r + 8, :] = yb
    for r in chunks(1, SMOOTH):
        for f in range(NT):
            base = SMOOTH * f + r - 1
            smoothed[base : base + 8, :] = smooth_rows(coeffs, start_field, r, f)


def sweep_rows(coeffs, field, left, right, start, bases, keep):
    rows = slice(start, start + 8)
    d, vx, vy, dz = (coeffs[i, rows, :] for i in range(4))
    a = 1.0 - 2.0 * d
    up, down = a * (d + vy), a * (d - vy)
    west, east = d + vx, d - vx
    h = shift_of(d, dz)
    lane = lax.broadcasted_iota(jnp.int32, (8, 128), 1)
    below = jnp.where(lane == 0, 0.0, dz)
    above = jnp.where(lane == 127, 0.0, dz)
    for pair in range(16):
        both = []
        for f in (2 * pair, 2 * pair + 1):
            center = field[f, rows, :]
            base = bases(f)
            both.append(
                up * field[f, start - 1 : start + 7, :]
                + down * field[f, start + 1 : start + 9, :]
                + west * left[base : base + 8, :]
                + east * right[base : base + 8, :]
                + below * pltpu.roll(center, 1, 1)
                + above * pltpu.roll(center, 127, 1)
            )
        keep(pair, *apply_inverse(pair, inverses(pair, h), *both))


def second_kernel(coeffs, start_field, left, right, next_field, smoothed):
    for r in chunks(1, SMOOTH):

        def keep(pair, a, b):
            for f, value in ((2 * pair, a), (2 * pair + 1, b)):
                next_field[f, r : r + 8, :] = start_field[f, r : r + 8, :] + value

        sweep_rows(coeffs, start_field, left, right, r, lambda f: SMOOTH * f + r - 1, keep)
    for r in chunks(2, ROWS):
        for f in range(NT):
            base = ROWS * f + r - 2
            smoothed[base : base + 8, :] = smooth_rows(coeffs, next_field, r, f)


def third_kernel(coeffs, start_field, next_field, left, right, blocks):
    for r in chunks(2, ROWS):
        spec = [None] * 17

        def keep(pair, a, b):
            a = start_field[2 * pair, r : r + 8, :] + a
            b = start_field[2 * pair + 1, r : r + 8, :] + b
            if pair == 0:
                spec[0], spec[16] = (a, None), (b, None)
            else:
                spec[pair] = (a, b)

        sweep_rows(coeffs, next_field, left, right, r, lambda f: ROWS * f + r - 2, keep)
        for n, value in enumerate(real_ifft(spec)):
            base = ROWS * (n % 4) + r - 2
            blocks[n // 4, base : base + 8, :] = value * (math.exp(-n * LOG_G) / NT)


def unpack_kernel(ids, blocks, out):
    odd_x = ids[1]
    for half in range(2):
        tracer = odd_x if half == 0 else 1 - odd_x
        for part in range(4):
            for step in range(4):
                out[step, tracer, ROWS * part : ROWS * part + ROWS, :] = blocks[
                    2 * part + half, ROWS * step : ROWS * step + ROWS, :
                ]


def f32(*shape):
    return jax.ShapeDtypeStruct(shape, jnp.float32)


def call(kernel, outs, scalars=0, inputs=1):
    vmem = pl.BlockSpec(memory_space=pltpu.VMEM)
    smem = pl.BlockSpec(memory_space=pltpu.SMEM)
    many = isinstance(outs, tuple)
    return pl.pallas_call(
        kernel,
        out_shape=outs,
        in_specs=[smem] * scalars + [vmem] * inputs,
        out_specs=(vmem,) * len(outs) if many else vmem,
        compiler_params=pltpu.CompilerParams(vmem_limit_bytes=VMEM),
    )


def shards(forcing, init_state, prev_last, diff_h, vel_x, vel_y, diff_z):
    pairs = x_neighbours()
    back = [(b, a) for a, b in pairs]
    axes = ("tm", "space")
    group, place = lax.axis_index("tm"), lax.axis_index("space")
    ids = jnp.stack([group // 2, (place // 16) % 2, group]).astype(jnp.int32)

    blocks, coeffs = call(pack_kernel, (f32(8, 4 * WIDE, 128), f32(4, 40, 128)), 1, 7)(
        ids,
        forcing.reshape(4, 2, 128, 128),
        init_state.reshape(2, 128, 128),
        prev_last.reshape(2, 128, 128),
        *(c.reshape(128, 128) for c in (diff_h, vel_x, vel_y, diff_z)),
    )
    gathered = lax.all_to_all(blocks, "tm", 0, 0)
    start_field, smoothed = call(first_kernel, (f32(NT, 40, 128), f32(NT * SMOOTH, 128)), 0, 2)(gathered, coeffs)
    left = lax.ppermute(smoothed, axes, pairs)
    right = lax.ppermute(smoothed, axes, back)
    next_field, smoothed = call(second_kernel, (f32(NT, 40, 128), f32(NT * ROWS, 128)), 0, 4)(
        coeffs, start_field, left, right
    )
    left = lax.ppermute(smoothed, axes, pairs)
    right = lax.ppermute(smoothed, axes, back)
    blocks = call(third_kernel, f32(8, 4 * ROWS, 128), 0, 5)(coeffs, start_field, next_field, left, right)
    gathered = lax.all_to_all(blocks, "tm", 0, 0)
    out = call(unpack_kernel, f32(4, 2, 128, 128), 1, 1)(ids, gathered)
    return out.reshape(forcing.shape)


def solution(mesh):
    return jax.shard_map(
        shards,
        mesh=mesh,
        in_specs=(
            P("tm", None, "space", None, None),
            P(None, "space", None, None),
            P(None, "space", None, None),
            P("space", None, None),
            P("space", None, None),
            P("space", None, None),
            P("space", None, None),
        ),
        out_specs=P("tm", None, "space", None, None),
        check_vma=False,
    )
```

time: 636 us -> 127 us (0.20)
  the two profiles are of different devices: /device:TPU:1 before, /device:TPU:37 now
where the time goes in v1:
time: 127 us; the launch traced here: 126 us
  blocking collectives  92.2 us (73%)
  waiting for transfers between devices  12.6 us (10%)
  starting transfers between devices  11.9 us (9%)
  local copies, waits for them, and re-layouts  6.13 us (5%)
  Pallas kernels  3.58 us (3%)
    all_to_all x2, blocking collectives, shards(): gathered = lax.all_to_all(blocks, 'tm', 0, 0)  92.2 us
    ppermute x2, waiting for transfers between devices, shards(): right = lax.ppermute(smoothed, axes, back)  10.8 us
    ppermute x2, starting transfers between devices, shards(): right = lax.ppermute(smoothed, axes, back)  7.83 us
    unnamed x14, local copies, waits for them, and re-layouts  6.13 us
    ppermute x2, starting transfers between devices, shards(): left = lax.ppermute(smoothed, axes, pairs)  4.05 us
  transfers between devices with their start and end apart: 4, of which 4 were waited for; matrix products, arithmetic and copies ran while one was open for 0% of the time, Pallas kernels for 0%

profile of v1, /device:TPU:37, one launch (start us, length us, event | category | flops | bytes accessed | tf_op | source)
XLA Modules:
  0.0 126.4 jit_solution(16839455802071889482)
XLA Ops:
  0.0 0.0 copy-start.3
  0.0 0.1 pad_add_fusion.ids
  0.1 0.8 copy-done.3
  0.8 0.0 copy-start
  0.8 1.0 copy-done
  1.9 0.0 copy-start.1
  1.9 0.9 copy-done.1
  2.8 0.0 copy-start.2
  2.8 0.9 copy-done.2
  3.7 0.0 copy-start.4
  3.7 0.8 copy-done.4
  4.5 0.0 copy-start.5
  4.5 0.8 copy-done.5
  5.4 0.0 copy-start.6
  5.4 0.8 copy-done.6
  6.2 0.6 shard_map.73
  6.8 54.3 %all_to_all.10.gathered = f32[8,144,128]{2,1,0:T(8,128)S(1)} all-to-all(f32[8,144,128]{2,1,0:T(8,128)S(1)} %get-tuple-element.12), channel_id=1, replica_groups=mesh['tm'=8,'space'=64] {'tm'}, dimensions={0} | all-to-all | bytes 1179648 | tf_op jit(solution)/shard_map/all_to_all | solution.py:275
  61.2 0.4 shard_map.74
  61.6 3.5 %collective-permute-start.1 = (f32[1088,128]{1,0:T(8,128)S(1)}, f32[1088,128]{1,0:T(8,128)S(1)}, u32[]{:S(2)}, u32[]{:S(2)}) collective-permute-start(f32[1088,128]{1,0:T(8,128)S(1)} %get-tuple-element.14), channel_id=1, source_target_pairs={{1,0},{2,1},{3,2},{4,3},{5,4},{6,5},{7,6},{8,7},{9,8},{10,9},{11,1... | collective-permute-start | bytes 1671176 | tf_op jit(solution)/shard_map/ppermute | solution.py:278
  65.2 2.0 %collective-permute-start = (f32[1088,128]{1,0:T(8,128)S(1)}, f32[1088,128]{1,0:T(8,128)S(1)}, u32[]{:S(2)}, u32[]{:S(2)}) collective-permute-start(f32[1088,128]{1,0:T(8,128)S(1)} %get-tuple-element.14), channel_id=1, source_target_pairs={{0,1},{1,2},{2,3},{3,4},{4,5},{5,6},{6,7},{7,8},{8,9},{9,10},{10,1... | collective-permute-start | bytes 1671176 | tf_op jit(solution)/shard_map/ppermute | solution.py:277
  67.2 5.6 %collective-permute-done.1.right = f32[1088,128]{1,0:T(8,128)S(1)} collective-permute-done((f32[1088,128]{1,0:T(8,128)S(1)}, f32[1088,128]{1,0:T(8,128)S(1)}, u32[]{:S(2)}, u32[]{:S(2)}) %collective-permute-start.1) | collective-permute-done | bytes 557088 | tf_op jit(solution)/shard_map/ppermute | solution.py:278
  72.8 0.9 collective-permute-done.left
  73.6 0.6 shard_map.75
  74.3 4.3 %collective-permute-start.3 = (f32[1024,128]{1,0:T(8,128)S(1)}, f32[1024,128]{1,0:T(8,128)S(1)}, u32[]{:S(2)}, u32[]{:S(2)}) collective-permute-start(f32[1024,128]{1,0:T(8,128)S(1)} %get-tuple-element.16), channel_id=1, source_target_pairs={{1,0},{2,1},{3,2},{4,3},{5,4},{6,5},{7,6},{8,7},{9,8},{10,9},{11,1... | collective-permute-start | bytes 1572872 | tf_op jit(solution)/shard_map/ppermute | solution.py:283
  78.6 2.0 %collective-permute-start.2 = (f32[1024,128]{1,0:T(8,128)S(1)}, f32[1024,128]{1,0:T(8,128)S(1)}, u32[]{:S(2)}, u32[]{:S(2)}) collective-permute-start(f32[1024,128]{1,0:T(8,128)S(1)} %get-tuple-element.16), channel_id=1, source_target_pairs={{0,1},{1,2},{2,3},{3,4},{4,5},{5,6},{6,7},{7,8},{8,9},{9,10},{10,1... | collective-permute-start | bytes 1572872 | tf_op jit(solution)/shard_map/ppermute | solution.py:282
  80.6 5.2 %collective-permute-done.3.right = f32[1024,128]{1,0:T(8,128)S(1)} collective-permute-done((f32[1024,128]{1,0:T(8,128)S(1)}, f32[1024,128]{1,0:T(8,128)S(1)}, u32[]{:S(2)}, u32[]{:S(2)}) %collective-permute-start.3) | collective-permute-done | bytes 524320 | tf_op jit(solution)/shard_map/ppermute | solution.py:283
  85.8 0.9 collective-permute-done.2.left
  86.7 0.5 shard_map.76
  87.2 37.8 %all_to_all.11.blocks = f32[8,128,128]{2,1,0:T(8,128)S(1)} all-to-all(f32[8,128,128]{2,1,0:T(8,128)S(1)} %shard_map.76), channel_id=1, replica_groups=mesh['tm'=8,'space'=64] {'tm'}, dimensions={0} | all-to-all | bytes 1048576 | tf_op jit(solution)/shard_map/all_to_all | solution.py:285
  125.1 1.4 %shard_map.77 = f32[4,2,128,128]{3,2,1,0:T(8,128)} custom-call(s32[3]{0:T(128)S(1)} %pad_add_fusion.ids, f32[8,128,128]{2,1,0:T(8,128)S(1)} %all_to_all.11.blocks), custom_call_target="tpu_custom_call" | custom-call | tf_op jit(solution)/shard_map/pallas_call | solution.py:286
Async XLA Ops:
  0.0 0.8 copy-start.3
  0.8 1.0 copy-start
  1.9 0.9 copy-start.1
  2.8 0.9 copy-start.2
  3.7 0.8 copy-start.4
  4.5 0.8 copy-start.5
  5.4 0.8 copy-start.6
  61.6 11.1 %collective-permute-start.1 = (f32[1088,128]{1,0:T(8,128)S(1)}, f32[1088,128]{1,0:T(8,128)S(1)}, u32[]{:S(2)}, u32[]{:S(2)}) collective-permute-start(f32[1088,128]{1,0:T(8,128)S(1)} %get-tuple-element.14), channel_id=1, source_target_pairs={{1,0},{2,1},{3,2},{4,3},{5,4},{6,5},{7,6},{8,7},{9,8},{10,9},{11,1... | collective-permute-start | bytes 1671176 | tf_op jit(solution)/shard_map/ppermute | solution.py:278
  65.2 8.5 %collective-permute-start = (f32[1088,128]{1,0:T(8,128)S(1)}, f32[1088,128]{1,0:T(8,128)S(1)}, u32[]{:S(2)}, u32[]{:S(2)}) collective-permute-start(f32[1088,128]{1,0:T(8,128)S(1)} %get-tuple-element.14), channel_id=1, source_target_pairs={{0,1},{1,2},{2,3},{3,4},{4,5},{5,6},{6,7},{7,8},{8,9},{9,10},{10,1... | collective-permute-start | bytes 1671176 | tf_op jit(solution)/shard_map/ppermute | solution.py:277
  74.3 11.5 %collective-permute-start.3 = (f32[1024,128]{1,0:T(8,128)S(1)}, f32[1024,128]{1,0:T(8,128)S(1)}, u32[]{:S(2)}, u32[]{:S(2)}) collective-permute-start(f32[1024,128]{1,0:T(8,128)S(1)} %get-tuple-element.16), channel_id=1, source_target_pairs={{1,0},{2,1},{3,2},{4,3},{5,4},{6,5},{7,6},{8,7},{9,8},{10,9},{11,1... | collective-permute-start | bytes 1572872 | tf_op jit(solution)/shard_map/ppermute | solution.py:283
  78.6 8.1 %collective-permute-start.2 = (f32[1024,128]{1,0:T(8,128)S(1)}, f32[1024,128]{1,0:T(8,128)S(1)}, u32[]{:S(2)}, u32[]{:S(2)}) collective-permute-start(f32[1024,128]{1,0:T(8,128)S(1)} %get-tuple-element.16), channel_id=1, source_target_pairs={{0,1},{1,2},{2,3},{3,4},{4,5},{5,6},{6,7},{7,8},{8,9},{9,10},{10,1... | collective-permute-start | bytes 1572872 | tf_op jit(solution)/shard_map/ppermute | solution.py:282

commit v2 on v1

--- a/solution.py
+++ b/solution.py
@@ -24,18 +24,24 @@
     return (y * 2 + z // half) * (CHIPS_X * half * CORES) + (x * half + z % half) * CORES + core
 
 
-def x_neighbours():
-    pairs = []
+def position():
+    group, place = lax.axis_index("tm"), lax.axis_index("space")
+    return group >> 1, group & 1, (place >> 4) & 1, place & 1
+
+
+def swaps():
+    near, far = [], []
     half = CHIPS_Z // 2
     for x in range(CHIPS_X):
         for y in range(CHIPS_Y):
             for z in range(CHIPS_Z):
-                here = flat_index(x, y, z, 0)
-                pairs.append((here, flat_index(x, y, z, 1)))
+                here, mate = flat_index(x, y, z, 0), flat_index(x, y, z, 1)
+                near += [(here, mate), (mate, here)]
                 step = x + 1 if z % half == half - 1 else x
                 if step < CHIPS_X:
-                    pairs.append((flat_index(x, y, z, 1), flat_index(step, y, (z + 1) % CHIPS_Z, 0)))
-    return pairs
+                    after = flat_index(step, y, (z + 1) % CHIPS_Z, 0)
+                    far += [(mate, after), (after, mate)]
+    return near, far
 
 
 def real_fft(values):
@@ -98,35 +104,59 @@
     return first * inv[0] + second * inv[1], second * inv[0] - first * inv[1]
 
 
-def pack_kernel(ids, forcing, init, prev, diff_h, vel_x, vel_y, diff_z, blocks, coeffs):
-    quarter, odd_x = ids[0], ids[1]
-    first = (ids[2] == 0).astype(jnp.float32)
-    for half in range(2):
-        tracer = odd_x if half == 0 else 1 - odd_x
-        for part in range(4):
-            dest = 2 * part + half
-            low, high = max(ROWS * part - 2, 0), min(ROWS * part + ROWS + 2, 128)
-            skip = low - (ROWS * part - 2)
-            for step in range(4):
-                value = forcing[step, tracer, low:high, :]
-                if step == 0:
-                    value = value + first * (init[tracer, low:high, :] - CORNER * prev[tracer, low:high, :])
-                base = WIDE * step
-                blocks[dest, base + skip : base + skip + high - low, :] = value
+def window(part):
+    low, high = max(ROWS * part - 2, 0), min(ROWS * part + ROWS + 2, 128)
+    return low, high, low - (ROWS * part - 2)
+
+
+def pack_kernel(forcing, init, prev, *refs):
+    sources, (blocks, coeffs), held, sems = refs[:4], refs[4:6], refs[6:13], refs[13]
+    quarter, own_half, odd_x, _ = position()
+    steps, values, firsts = held[0], held[1:5], held[5:7]
+    loads = [pltpu.make_async_copy(forcing.at[step], steps.at[step], sems.at[step]) for step in range(4)]
+    others = [pltpu.make_async_copy(source, values[i], sems.at[4 + i]) for i, source in enumerate(sources)]
+    holds_first = jnp.logical_and(quarter == 0, own_half == 0)
+    for copy in loads + others:
+        copy.start()
+
+    @pl.when(holds_first)
+    def _():
+        pair = [pltpu.make_async_copy(a, firsts[i], sems.at[8 + i]) for i, a in enumerate((init, prev))]
+        for copy in pair:
+            copy.start()
+        for copy in pair:
+            copy.wait()
+
+    loads[0].wait()
+
+    @pl.when(holds_first)
+    def _():
+        steps[0] += firsts[0][...] - CORNER * firsts[1][...]
+
+    for step in range(4):
+        if step:
+            loads[step].wait()
+        for half in range(2):
+            tracer = odd_x if half == 0 else 1 - odd_x
+            for part in range(4):
+                low, high, skip = window(part)
+                rest = WIDE - skip - (high - low)
+                dest, base = 2 * part + half, WIDE * step
+                blocks[dest, base + skip : base + skip + high - low, :] = steps[step, tracer, low:high, :]
                 if skip:
                     blocks[dest, base : base + skip, :] = jnp.zeros((skip, 128), jnp.float32)
-                rest = WIDE - skip - (high - low)
                 if rest:
                     blocks[dest, base + WIDE - rest : base + WIDE, :] = jnp.zeros((rest, 128), jnp.float32)
+    for copy in others:
+        copy.wait()
     for part in range(4):
 
         @pl.when(quarter == part)
         def _():
-            low, high = max(ROWS * part - 2, 0), min(ROWS * part + ROWS + 2, 128)
-            skip = low - (ROWS * part - 2)
+            low, high, skip = window(part)
             if part in (0, 3):
                 coeffs[...] = jnp.zeros(coeffs.shape, jnp.float32)
-            for i, ref in enumerate((diff_h, vel_x, vel_y, diff_z)):
+            for i, ref in enumerate(values):
                 coeffs[i, skip : skip + high - low, :] = ref[low:high, :]
 
 
@@ -172,12 +202,13 @@
             smoothed[base : base + 8, :] = smooth_rows(coeffs, start_field, r, f)
 
 
-def sweep_rows(coeffs, field, left, right, start, bases, keep):
+def sweep_rows(coeffs, field, near, far, start, bases, keep):
     rows = slice(start, start + 8)
     d, vx, vy, dz = (coeffs[i, rows, :] for i in range(4))
     a = 1.0 - 2.0 * d
     up, down = a * (d + vy), a * (d - vy)
-    west, east = d + vx, d - vx
+    sign = (2 * position()[3] - 1).astype(jnp.float32)
+    beside, across = d + sign * vx, d - sign * vx
     h = shift_of(d, dz)
     lane = lax.broadcasted_iota(jnp.int32, (8, 128), 1)
     below = jnp.where(lane == 0, 0.0, dz)
@@ -190,29 +221,29 @@
             both.append(
                 up * field[f, start - 1 : start + 7, :]
                 + down * field[f, start + 1 : start + 9, :]
-                + west * left[base : base + 8, :]
-                + east * right[base : base + 8, :]
+                + beside * near[base : base + 8, :]
+                + across * far[base : base + 8, :]
                 + below * pltpu.roll(center, 1, 1)
                 + above * pltpu.roll(center, 127, 1)
             )
         keep(pair, *apply_inverse(pair, inverses(pair, h), *both))
 
 
-def second_kernel(coeffs, start_field, left, right, next_field, smoothed):
+def second_kernel(coeffs, start_field, near, far, next_field, smoothed):
     for r in chunks(1, SMOOTH):
 
         def keep(pair, a, b):
             for f, value in ((2 * pair, a), (2 * pair + 1, b)):
                 next_field[f, r : r + 8, :] = start_field[f, r : r + 8, :] + value
 
-        sweep_rows(coeffs, start_field, left, right, r, lambda f: SMOOTH * f + r - 1, keep)
+        sweep_rows(coeffs, start_field, near, far, r, lambda f: SMOOTH * f + r - 1, keep)
     for r in chunks(2, ROWS):
         for f in range(NT):
             base = ROWS * f + r - 2
             smoothed[base : base + 8, :] = smooth_rows(coeffs, next_field, r, f)
 
 
-def third_kernel(coeffs, start_field, next_field, left, right, blocks):
+def third_kernel(coeffs, start_field, next_field, near, far, blocks):
     for r in chunks(2, ROWS):
         spec = [None] * 17
 
@@ -224,66 +255,71 @@
             else:
                 spec[pair] = (a, b)
 
-        sweep_rows(coeffs, next_field, left, right, r, lambda f: ROWS * f + r - 2, keep)
+        sweep_rows(coeffs, next_field, near, far, r, lambda f: ROWS * f + r - 2, keep)
         for n, value in enumerate(real_ifft(spec)):
             base = ROWS * (n % 4) + r - 2
             blocks[n // 4, base : base + 8, :] = value * (math.exp(-n * LOG_G) / NT)
 
 
-def unpack_kernel(ids, blocks, out):
-    odd_x = ids[1]
+def unpack_kernel(gathered, out, sems):
+    odd_x = position()[2]
+    copies = []
     for half in range(2):
         tracer = odd_x if half == 0 else 1 - odd_x
         for part in range(4):
-            for step in range(4):
-                out[step, tracer, ROWS * part : ROWS * part + ROWS, :] = blocks[
-                    2 * part + half, ROWS * step : ROWS * step + ROWS, :
-                ]
+            block = 2 * part + half
+            target = out.at[:, tracer, pl.ds(ROWS * part, ROWS), :]
+            copies.append(pltpu.make_async_copy(gathered.at[block], target, sems.at[block]))
+    for copy in copies:
+        copy.start()
+    for copy in copies:
+        copy.wait()
 
 
 def f32(*shape):
     return jax.ShapeDtypeStruct(shape, jnp.float32)
 
 
-def call(kernel, outs, scalars=0, inputs=1):
+def call(kernel, outs, inputs=1, far_in=False, far_out=False, scratch=()):
     vmem = pl.BlockSpec(memory_space=pltpu.VMEM)
-    smem = pl.BlockSpec(memory_space=pltpu.SMEM)
-    many = isinstance(outs, tuple)
+    hbm = pl.BlockSpec(memory_space=pltpu.HBM)
+    out_spec = hbm if far_out else vmem
     return pl.pallas_call(
         kernel,
         out_shape=outs,
-        in_specs=[smem] * scalars + [vmem] * inputs,
-        out_specs=(vmem,) * len(outs) if many else vmem,
+        in_specs=[hbm if far_in else vmem] * inputs,
+        out_specs=(out_spec,) * len(outs) if isinstance(outs, tuple) else out_spec,
+        scratch_shapes=list(scratch),
         compiler_params=pltpu.CompilerParams(vmem_limit_bytes=VMEM),
     )
 
 
 def shards(forcing, init_state, prev_last, diff_h, vel_x, vel_y, diff_z):
-    pairs = x_neighbours()
-    back = [(b, a) for a, b in pairs]
+    near, far = swaps()
     axes = ("tm", "space")
-    group, place = lax.axis_index("tm"), lax.axis_index("space")
-    ids = jnp.stack([group // 2, (place // 16) % 2, group]).astype(jnp.int32)
-
-    blocks, coeffs = call(pack_kernel, (f32(8, 4 * WIDE, 128), f32(4, 40, 128)), 1, 7)(
-        ids,
+    operands = (
         forcing.reshape(4, 2, 128, 128),
         init_state.reshape(2, 128, 128),
         prev_last.reshape(2, 128, 128),
         *(c.reshape(128, 128) for c in (diff_h, vel_x, vel_y, diff_z)),
     )
+    order = (0, 3, 4, 5, 6, 1, 2)
+    scratch = [pltpu.VMEM(operands[i].shape, jnp.float32) for i in order] + [pltpu.SemaphoreType.DMA((10,))]
+    blocks, coeffs = call(pack_kernel, (f32(8, 4 * WIDE, 128), f32(4, 40, 128)), 7, far_in=True, scratch=scratch)(
+        *(pltpu.with_memory_space_constraint(a, pltpu.HBM) for a in operands)
+    )
     gathered = lax.all_to_all(blocks, "tm", 0, 0)
-    start_field, smoothed = call(first_kernel, (f32(NT, 40, 128), f32(NT * SMOOTH, 128)), 0, 2)(gathered, coeffs)
-    left = lax.ppermute(smoothed, axes, pairs)
-    right = lax.ppermute(smoothed, axes, back)
-    next_field, smoothed = call(second_kernel, (f32(NT, 40, 128), f32(NT * ROWS, 128)), 0, 4)(
-        coeffs, start_field, left, right
-    )
-    left = lax.ppermute(smoothed, axes, pairs)
-    right = lax.ppermute(smoothed, axes, back)
-    blocks = call(third_kernel, f32(8, 4 * ROWS, 128), 0, 5)(coeffs, start_field, next_field, left, right)
-    gathered = lax.all_to_all(blocks, "tm", 0, 0)
-    out = call(unpack_kernel, f32(4, 2, 128, 128), 1, 1)(ids, gathered)
+    start_field, smoothed = call(first_kernel, (f32(NT, 40, 128), f32(NT * SMOOTH, 128)), 2)(gathered, coeffs)
+    across = lax.ppermute(smoothed, axes, far)
+    beside = lax.ppermute(smoothed, axes, near)
+    next_field, smoothed = call(second_kernel, (f32(NT, 40, 128), f32(NT * ROWS, 128)), 4)(
+        coeffs, start_field, beside, across
+    )
+    across = lax.ppermute(smoothed, axes, far)
+    beside = lax.ppermute(smoothed, axes, near)
+    blocks = call(third_kernel, f32(8, 4 * ROWS, 128), 5)(coeffs, start_field, next_field, beside, across)
+    gathered = lax.all_to_all(blocks, "tm", 0, 0).reshape(8, 4, ROWS, 128)
+    out = call(unpack_kernel, f32(4, 2, 128, 128), 1, far_out=True, scratch=[pltpu.SemaphoreType.DMA((8,))])(gathered)
     return out.reshape(forcing.shape)
 
 

time: 127 us -> 117 us (0.921)
  local copies, waits for them, and re-layouts: 6.13 us -> 0 us
  starting transfers between devices: 11.9 us -> 10.6 us
  waiting for transfers between devices: 12.6 us -> 11.3 us
    all_to_all x2 -> x1, blocking collectives: 92.2 us -> 54.1 us  [shards(): gathered = lax.all_to_all(blocks, 'tm', 0, 0)]
    all_to_all x0 -> x1, blocking collectives: none -> 37.1 us  [shards(): gathered = lax.all_to_all(blocks, 'tm', 0, 0).reshape(8, 4, ROWS, 128)]
    unnamed x14 -> x0, local copies, waits for them, and re-layouts: 6.13 us -> none
  transfers between devices with their start and end apart: 4 -> 4, of which waited for: 4 -> 2; matrix products, arithmetic and copies ran while one was open for 0% -> 0% of each run, Pallas kernels for 0% -> 0%
where the time goes in v2:
time: 117 us
  blocking collectives  91.2 us (78%)
  waiting for transfers between devices  11.3 us (10%)
  starting transfers between devices  10.6 us (9%)
  Pallas kernels  3.91 us (3%)
    all_to_all x1, blocking collectives, shards(): gathered = lax.all_to_all(blocks, 'tm', 0, 0)  54.1 us
    all_to_all x1, blocking collectives, shards(): gathered = lax.all_to_all(blocks, 'tm', 0, 0).reshape(8, 4, ROWS, 128)  37.1 us
    ppermute x2, waiting for transfers between devices, shards(): across = lax.ppermute(smoothed, axes, far)  11.3 us
    ppermute x2, starting transfers between devices, shards(): beside = lax.ppermute(smoothed, axes, near)  6.79 us
    ppermute x2, starting transfers between devices, shards(): across = lax.ppermute(smoothed, axes, far)  3.84 us
  transfers between devices with their start and end apart: 4, of which 2 were waited for; matrix products, arithmetic and copies ran while one was open for 0% of the time, Pallas kernels for 0%

profile of v2, /device:TPU:37, one launch (start us, length us, event | category | flops | bytes accessed | tf_op | source)
XLA Modules:
  0.0 117.0 jit_solution(11067823481025965995)
XLA Ops:
  0.0 1.5 %shard_map.73 = (f32[8,144,128]{2,1,0:T(8,128)S(1)}, f32[4,40,128]{2,1,0:T(8,128)S(1)}) custom-call(f32[4,2,128,128]{3,2,1,0:T(8,128)} %bitcast.12, f32[2,128,128]{2,1,0:T(8,128)} %bitcast.13, f32[2,128,128]{2,1,0:T(8,128)} %bitcast.14, f32[128,128]{1,0:T(8,128)} %bitcast.15, f32[128,128]{1,0:T(8,128)} %bitcast.16, f32[128,128]{1,0:T(8,128)} %bitcast.17, ...), custom_call_target="tpu_custom_call" | custom-call | tf_op jit(solution)/shard_map/pallas_call | solution.py:308
  1.5 54.1 %all_to_all.10.gathered = f32[8,144,128]{2,1,0:T(8,128)S(1)} all-to-all(f32[8,144,128]{2,1,0:T(8,128)S(1)} %get-tuple-element.12), channel_id=1, replica_groups=mesh['tm'=8,'space'=64] {'tm'}, dimensions={0} | all-to-all | bytes 1179648 | tf_op jit(solution)/shard_map/all_to_all | solution.py:311
  55.6 0.4 shard_map.74
  56.0 1.9 %collective-permute-start.1 = (f32[1088,128]{1,0:T(8,128)S(1)}, f32[1088,128]{1,0:T(8,128)S(1)}, u32[]{:S(2)}, u32[]{:S(2)}) collective-permute-start(f32[1088,128]{1,0:T(8,128)S(1)} %get-tuple-element.14), channel_id=1, source_target_pairs={{1,2},{2,1},{3,4},{4,3},{5,6},{6,5},{7,8},{8,7},{9,10},{10,9},{11,... | collective-permute-start | bytes 1671176 | tf_op jit(solution)/shard_map/ppermute | solution.py:313
  58.0 3.5 %collective-permute-start = (f32[1088,128]{1,0:T(8,128)S(1)}, f32[1088,128]{1,0:T(8,128)S(1)}, u32[]{:S(2)}, u32[]{:S(2)}) collective-permute-start(f32[1088,128]{1,0:T(8,128)S(1)} %get-tuple-element.14), channel_id=1, source_target_pairs={{0,1},{1,0},{2,3},{3,2},{4,5},{5,4},{6,7},{7,6},{8,9},{9,8},{10,11... | collective-permute-start | bytes 1671176 | tf_op jit(solution)/shard_map/ppermute | solution.py:314
  61.5 5.7 %collective-permute-done.1.far = f32[1088,128]{1,0:T(8,128)S(1)} collective-permute-done((f32[1088,128]{1,0:T(8,128)S(1)}, f32[1088,128]{1,0:T(8,128)S(1)}, u32[]{:S(2)}, u32[]{:S(2)}) %collective-permute-start.1) | collective-permute-done | bytes 557088 | tf_op jit(solution)/shard_map/ppermute | solution.py:313
  67.2 0.0 collective-permute-done.near
  67.2 0.6 shard_map.75
  67.8 1.9 %collective-permute-start.3 = (f32[1024,128]{1,0:T(8,128)S(1)}, f32[1024,128]{1,0:T(8,128)S(1)}, u32[]{:S(2)}, u32[]{:S(2)}) collective-permute-start(f32[1024,128]{1,0:T(8,128)S(1)} %get-tuple-element.16), channel_id=1, source_target_pairs={{1,2},{2,1},{3,4},{4,3},{5,6},{6,5},{7,8},{8,7},{9,10},{10,9},{11,... | collective-permute-start | bytes 1572872 | tf_op jit(solution)/shard_map/ppermute | solution.py:318
  69.7 3.2 %collective-permute-start.2 = (f32[1024,128]{1,0:T(8,128)S(1)}, f32[1024,128]{1,0:T(8,128)S(1)}, u32[]{:S(2)}, u32[]{:S(2)}) collective-permute-start(f32[1024,128]{1,0:T(8,128)S(1)} %get-tuple-element.16), channel_id=1, source_target_pairs={{0,1},{1,0},{2,3},{3,2},{4,5},{5,4},{6,7},{7,6},{8,9},{9,8},{10,11... | collective-permute-start | bytes 1572872 | tf_op jit(solution)/shard_map/ppermute | solution.py:319
  73.0 5.6 %collective-permute-done.3.far = f32[1024,128]{1,0:T(8,128)S(1)} collective-permute-done((f32[1024,128]{1,0:T(8,128)S(1)}, f32[1024,128]{1,0:T(8,128)S(1)}, u32[]{:S(2)}, u32[]{:S(2)}) %collective-permute-start.3) | collective-permute-done | bytes 524320 | tf_op jit(solution)/shard_map/ppermute | solution.py:318
  78.6 0.0 collective-permute-done.2.near
  78.6 0.5 shard_map.76
  79.1 37.1 %all_to_all.11 = f32[8,128,128]{2,1,0:T(8,128)S(1)} all-to-all(f32[8,128,128]{2,1,0:T(8,128)S(1)} %shard_map.76), channel_id=1, replica_groups=mesh['tm'=8,'space'=64] {'tm'}, dimensions={0} | all-to-all | bytes 1048576 | tf_op jit(solution)/shard_map/all_to_all | solution.py:321
  116.2 0.8 shard_map.77
Async XLA Ops:
  56.0 11.1 %collective-permute-start.1 = (f32[1088,128]{1,0:T(8,128)S(1)}, f32[1088,128]{1,0:T(8,128)S(1)}, u32[]{:S(2)}, u32[]{:S(2)}) collective-permute-start(f32[1088,128]{1,0:T(8,128)S(1)} %get-tuple-element.14), channel_id=1, source_target_pairs={{1,2},{2,1},{3,4},{4,3},{5,6},{6,5},{7,8},{8,7},{9,10},{10,9},{11,... | collective-permute-start | bytes 1671176 | tf_op jit(solution)/shard_map/ppermute | solution.py:313
  58.0 9.2 %collective-permute-start = (f32[1088,128]{1,0:T(8,128)S(1)}, f32[1088,128]{1,0:T(8,128)S(1)}, u32[]{:S(2)}, u32[]{:S(2)}) collective-permute-start(f32[1088,128]{1,0:T(8,128)S(1)} %get-tuple-element.14), channel_id=1, source_target_pairs={{0,1},{1,0},{2,3},{3,2},{4,5},{5,4},{6,7},{7,6},{8,9},{9,8},{10,11... | collective-permute-start | bytes 1671176 | tf_op jit(solution)/shard_map/ppermute | solution.py:314
  67.8 10.8 %collective-permute-start.3 = (f32[1024,128]{1,0:T(8,128)S(1)}, f32[1024,128]{1,0:T(8,128)S(1)}, u32[]{:S(2)}, u32[]{:S(2)}) collective-permute-start(f32[1024,128]{1,0:T(8,128)S(1)} %get-tuple-element.16), channel_id=1, source_target_pairs={{1,2},{2,1},{3,4},{4,3},{5,6},{6,5},{7,8},{8,7},{9,10},{10,9},{11,... | collective-permute-start | bytes 1572872 | tf_op jit(solution)/shard_map/ppermute | solution.py:318
  69.7 8.9 %collective-permute-start.2 = (f32[1024,128]{1,0:T(8,128)S(1)}, f32[1024,128]{1,0:T(8,128)S(1)}, u32[]{:S(2)}, u32[]{:S(2)}) collective-permute-start(f32[1024,128]{1,0:T(8,128)S(1)} %get-tuple-element.16), channel_id=1, source_target_pairs={{0,1},{1,0},{2,3},{3,2},{4,5},{5,4},{6,7},{7,6},{8,9},{9,8},{10,11... | collective-permute-start | bytes 1572872 | tf_op jit(solution)/shard_map/ppermute | solution.py:319

commit v3 on v2

--- a/solution.py
+++ b/solution.py
@@ -26,7 +26,29 @@
 
 def position():
     group, place = lax.axis_index("tm"), lax.axis_index("space")
-    return group >> 1, group & 1, (place >> 4) & 1, place & 1
+    return group >> 1, group & 1, (place >> 4) & 1, place & 1, (place >> 1) & 7
+
+
+THERE = (16449171, 477046, 13642849, 7670213, 9222671, 4329752, 11130092, 4187066)
+BACK = (12686257, 15687872, 4709462, 3586597, 10243739, 11053039, 7473418, 1668476)
+
+
+def slots_at(places, z):
+    return [(place >> (3 * z)) & 7 for place in places]
+
+
+def exchange(places, blocks):
+    half = CHIPS_Z // 2
+    groups = []
+    for x in range(CHIPS_X):
+        for z in range(half):
+            slots = slots_at(places, z)
+            for core in range(CORES):
+                members = [0] * 8
+                for group, slot in enumerate(slots):
+                    members[slot] = flat_index(x, group // 2, z + half * (group % 2), core)
+                groups.append(members)
+    return lax.all_to_all(blocks, ("tm", "space"), 0, 0, axis_index_groups=groups)
 
 
 def swaps():
@@ -111,7 +133,8 @@
 
 def pack_kernel(forcing, init, prev, *refs):
     sources, (blocks, coeffs), held, sems = refs[:4], refs[4:6], refs[6:13], refs[13]
-    quarter, own_half, odd_x, _ = position()
+    quarter, own_half, odd_x, _, z = position()
+    slots = slots_at(THERE, z)
     steps, values, firsts = held[0], held[1:5], held[5:7]
     loads = [pltpu.make_async_copy(forcing.at[step], steps.at[step], sems.at[step]) for step in range(4)]
     others = [pltpu.make_async_copy(source, values[i], sems.at[4 + i]) for i, source in enumerate(sources)]
@@ -141,7 +164,7 @@
             for part in range(4):
                 low, high, skip = window(part)
                 rest = WIDE - skip - (high - low)
-                dest, base = 2 * part + half, WIDE * step
+                dest, base = slots[2 * part + half], WIDE * step
                 blocks[dest, base + skip : base + skip + high - low, :] = steps[step, tracer, low:high, :]
                 if skip:
                     blocks[dest, base : base + skip, :] = jnp.zeros((skip, 128), jnp.float32)
@@ -183,11 +206,12 @@
 
 
 def first_kernel(gathered, coeffs, start_field, smoothed):
+    slots = slots_at(THERE, position()[4])
     for r in chunks(0, WIDE):
         values = []
         for n in range(NT):
             base = WIDE * (n % 4) + r
-            value = gathered[n // 4, base : base + 8, :]
+            value = gathered[slots[n // 4], base : base + 8, :]
             values.append(value * math.exp(n * LOG_G) if n else value)
         spec = real_fft(values)
         h = shift_of(coeffs[0, r : r + 8, :], coeffs[3, r : r + 8, :])
@@ -244,6 +268,7 @@
 
 
 def third_kernel(coeffs, start_field, next_field, near, far, blocks):
+    slots = slots_at(BACK, position()[4])
     for r in chunks(2, ROWS):
         spec = [None] * 17
 
@@ -258,18 +283,19 @@
         sweep_rows(coeffs, next_field, near, far, r, lambda f: ROWS * f + r - 2, keep)
         for n, value in enumerate(real_ifft(spec)):
             base = ROWS * (n % 4) + r - 2
-            blocks[n // 4, base : base + 8, :] = value * (math.exp(-n * LOG_G) / NT)
+            blocks[slots[n // 4], base : base + 8, :] = value * (math.exp(-n * LOG_G) / NT)
 
 
 def unpack_kernel(gathered, out, sems):
-    odd_x = position()[2]
+    _, _, odd_x, _, z = position()
+    slots = slots_at(BACK, z)
     copies = []
     for half in range(2):
         tracer = odd_x if half == 0 else 1 - odd_x
         for part in range(4):
             block = 2 * part + half
             target = out.at[:, tracer, pl.ds(ROWS * part, ROWS), :]
-            copies.append(pltpu.make_async_copy(gathered.at[block], target, sems.at[block]))
+            copies.append(pltpu.make_async_copy(gathered.at[slots[block]], target, sems.at[block]))
     for copy in copies:
         copy.start()
     for copy in copies:
@@ -308,7 +334,7 @@
     blocks, coeffs = call(pack_kernel, (f32(8, 4 * WIDE, 128), f32(4, 40, 128)), 7, far_in=True, scratch=scratch)(
         *(pltpu.with_memory_space_constraint(a, pltpu.HBM) for a in operands)
     )
-    gathered = lax.all_to_all(blocks, "tm", 0, 0)
+    gathered = exchange(THERE, blocks)
     start_field, smoothed = call(first_kernel, (f32(NT, 40, 128), f32(NT * SMOOTH, 128)), 2)(gathered, coeffs)
     across = lax.ppermute(smoothed, axes, far)
     beside = lax.ppermute(smoothed, axes, near)
@@ -318,7 +344,7 @@
     across = lax.ppermute(smoothed, axes, far)
     beside = lax.ppermute(smoothed, axes, near)
     blocks = call(third_kernel, f32(8, 4 * ROWS, 128), 5)(coeffs, start_field, next_field, beside, across)
-    gathered = lax.all_to_all(blocks, "tm", 0, 0).reshape(8, 4, ROWS, 128)
+    gathered = exchange(BACK, blocks).reshape(8, 4, ROWS, 128)
     out = call(unpack_kernel, f32(4, 2, 128, 128), 1, far_out=True, scratch=[pltpu.SemaphoreType.DMA((8,))])(gathered)
     return out.reshape(forcing.shape)
 

time: 117 us -> 106 us (0.906)
  the two profiles are of different devices: /device:TPU:37 before, /device:TPU:109 now
where the time goes in v3:
time: 106 us
  blocking collectives  65.6 us (62%)
  starting transfers between devices  26.2 us (25%)
  waiting for transfers between devices  10.2 us (10%)
  Pallas kernels  3.68 us (3%)
    all_to_all x2, blocking collectives, exchange(): lax.all_to_all(blocks, ('tm', 'space'), 0, 0, axis_index_groups=groups)  65.6 us
    ppermute x2, starting transfers between devices, shards(): across = lax.ppermute(smoothed, axes, far)  22.4 us
    ppermute x2, waiting for transfers between devices, shards(): across = lax.ppermute(smoothed, axes, far)  10.2 us
    ppermute x2, starting transfers between devices, shards(): beside = lax.ppermute(smoothed, axes, near)  3.84 us
  transfers between devices with their start and end apart: 4, of which 2 were waited for; matrix products, arithmetic and copies ran while one was open for 0% of the time, Pallas kernels for 0%

profile of v3, /device:TPU:109, one launch (start us, length us, event | category | flops | bytes accessed | tf_op | source)
XLA Modules:
  0.0 105.8 jit_solution(1258312938295225587)
XLA Ops:
  0.0 1.2 %shard_map.73 = (f32[8,144,128]{2,1,0:T(8,128)S(1)}, f32[4,40,128]{2,1,0:T(8,128)S(1)}) custom-call(f32[4,2,128,128]{3,2,1,0:T(8,128)} %bitcast.12, f32[2,128,128]{2,1,0:T(8,128)} %bitcast.13, f32[2,128,128]{2,1,0:T(8,128)} %bitcast.14, f32[128,128]{1,0:T(8,128)} %bitcast.15, f32[128,128]{1,0:T(8,128)} %bitcast.16, f32[128,128]{1,0:T(8,128)} %bitcast.17, ...), custom_call_target="tpu_custom_call" | custom-call | tf_op jit(solution)/shard_map/pallas_call | solution.py:334
  1.3 27.9 %all_to_all.10.gathered = f32[8,144,128]{2,1,0:T(8,128)S(1)} all-to-all(f32[8,144,128]{2,1,0:T(8,128)S(1)} %get-tuple-element.12), channel_id=1, replica_groups={{320,128,448,0,384,192,64,256},{321,129,449,1,385,193,65,257},{194,258,..., dimensions={0} | all-to-all | bytes 1179648 | tf_op jit(solution)/shard_map/all_to_all | solution.py:51
  29.1 0.5 shard_map.74
  29.6 15.0 %collective-permute-start.1 = (f32[1088,128]{1,0:T(8,128)S(1)}, f32[1088,128]{1,0:T(8,128)S(1)}, u32[]{:S(2)}, u32[]{:S(2)}) collective-permute-start(f32[1088,128]{1,0:T(8,128)S(1)} %get-tuple-element.14), channel_id=1, source_target_pairs={{1,2},{2,1},{3,4},{4,3},{5,6},{6,5},{7,8},{8,7},{9,10},{10,9},{11,... | collective-permute-start | bytes 1671176 | tf_op jit(solution)/shard_map/ppermute | solution.py:339
  44.6 1.9 %collective-permute-start = (f32[1088,128]{1,0:T(8,128)S(1)}, f32[1088,128]{1,0:T(8,128)S(1)}, u32[]{:S(2)}, u32[]{:S(2)}) collective-permute-start(f32[1088,128]{1,0:T(8,128)S(1)} %get-tuple-element.14), channel_id=1, source_target_pairs={{0,1},{1,0},{2,3},{3,2},{4,5},{5,4},{6,7},{7,6},{8,9},{9,8},{10,11... | collective-permute-start | bytes 1671176 | tf_op jit(solution)/shard_map/ppermute | solution.py:340
  46.5 5.3 %collective-permute-done.1.far = f32[1088,128]{1,0:T(8,128)S(1)} collective-permute-done((f32[1088,128]{1,0:T(8,128)S(1)}, f32[1088,128]{1,0:T(8,128)S(1)}, u32[]{:S(2)}, u32[]{:S(2)}) %collective-permute-start.1) | collective-permute-done | bytes 557088 | tf_op jit(solution)/shard_map/ppermute | solution.py:339
  51.8 0.0 collective-permute-done.near
  51.8 0.6 shard_map.75
  52.4 7.4 %collective-permute-start.3 = (f32[1024,128]{1,0:T(8,128)S(1)}, f32[1024,128]{1,0:T(8,128)S(1)}, u32[]{:S(2)}, u32[]{:S(2)}) collective-permute-start(f32[1024,128]{1,0:T(8,128)S(1)} %get-tuple-element.16), channel_id=1, source_target_pairs={{1,2},{2,1},{3,4},{4,3},{5,6},{6,5},{7,8},{8,7},{9,10},{10,9},{11,... | collective-permute-start | bytes 1572872 | tf_op jit(solution)/shard_map/ppermute | solution.py:344
  59.8 1.9 %collective-permute-start.2 = (f32[1024,128]{1,0:T(8,128)S(1)}, f32[1024,128]{1,0:T(8,128)S(1)}, u32[]{:S(2)}, u32[]{:S(2)}) collective-permute-start(f32[1024,128]{1,0:T(8,128)S(1)} %get-tuple-element.16), channel_id=1, source_target_pairs={{0,1},{1,0},{2,3},{3,2},{4,5},{5,4},{6,7},{7,6},{8,9},{9,8},{10,11... | collective-permute-start | bytes 1572872 | tf_op jit(solution)/shard_map/ppermute | solution.py:345
  61.8 4.9 %collective-permute-done.3.far = f32[1024,128]{1,0:T(8,128)S(1)} collective-permute-done((f32[1024,128]{1,0:T(8,128)S(1)}, f32[1024,128]{1,0:T(8,128)S(1)}, u32[]{:S(2)}, u32[]{:S(2)}) %collective-permute-start.3) | collective-permute-done | bytes 524320 | tf_op jit(solution)/shard_map/ppermute | solution.py:344
  66.7 0.0 collective-permute-done.2.near
  66.7 0.5 shard_map.76
  67.2 37.7 %all_to_all.11 = f32[8,128,128]{2,1,0:T(8,128)S(1)} all-to-all(f32[8,128,128]{2,1,0:T(8,128)S(1)} %shard_map.76), channel_id=1, replica_groups={{64,0,384,256,448,192,128,320},{65,1,385,257,449,193,129,321},{66,386,1..., dimensions={0} | all-to-all | bytes 1048576 | tf_op jit(solution)/shard_map/all_to_all | solution.py:51
  104.9 0.8 shard_map.77
Async XLA Ops:
  29.6 22.2 %collective-permute-start.1 = (f32[1088,128]{1,0:T(8,128)S(1)}, f32[1088,128]{1,0:T(8,128)S(1)}, u32[]{:S(2)}, u32[]{:S(2)}) collective-permute-start(f32[1088,128]{1,0:T(8,128)S(1)} %get-tuple-element.14), channel_id=1, source_target_pairs={{1,2},{2,1},{3,4},{4,3},{5,6},{6,5},{7,8},{8,7},{9,10},{10,9},{11,... | collective-permute-start | bytes 1671176 | tf_op jit(solution)/shard_map/ppermute | solution.py:339
  44.6 7.2 %collective-permute-start = (f32[1088,128]{1,0:T(8,128)S(1)}, f32[1088,128]{1,0:T(8,128)S(1)}, u32[]{:S(2)}, u32[]{:S(2)}) collective-permute-start(f32[1088,128]{1,0:T(8,128)S(1)} %get-tuple-element.14), channel_id=1, source_target_pairs={{0,1},{1,0},{2,3},{3,2},{4,5},{5,4},{6,7},{7,6},{8,9},{9,8},{10,11... | collective-permute-start | bytes 1671176 | tf_op jit(solution)/shard_map/ppermute | solution.py:340
  52.4 14.3 %collective-permute-start.3 = (f32[1024,128]{1,0:T(8,128)S(1)}, f32[1024,128]{1,0:T(8,128)S(1)}, u32[]{:S(2)}, u32[]{:S(2)}) collective-permute-start(f32[1024,128]{1,0:T(8,128)S(1)} %get-tuple-element.16), channel_id=1, source_target_pairs={{1,2},{2,1},{3,4},{4,3},{5,6},{6,5},{7,8},{8,7},{9,10},{10,9},{11,... | collective-permute-start | bytes 1572872 | tf_op jit(solution)/shard_map/ppermute | solution.py:344
  59.8 6.9 %collective-permute-start.2 = (f32[1024,128]{1,0:T(8,128)S(1)}, f32[1024,128]{1,0:T(8,128)S(1)}, u32[]{:S(2)}, u32[]{:S(2)}) collective-permute-start(f32[1024,128]{1,0:T(8,128)S(1)} %get-tuple-element.16), channel_id=1, source_target_pairs={{0,1},{1,0},{2,3},{3,2},{4,5},{5,4},{6,7},{7,6},{8,9},{9,8},{10,11... | collective-permute-start | bytes 1572872 | tf_op jit(solution)/shard_map/ppermute | solution.py:345

commit v4 on v3

--- a/solution.py
+++ b/solution.py
@@ -29,8 +29,8 @@
     return group >> 1, group & 1, (place >> 4) & 1, place & 1, (place >> 1) & 7
 
 
-THERE = (16449171, 477046, 13642849, 7670213, 9222671, 4329752, 11130092, 4187066)
-BACK = (12686257, 15687872, 4709462, 3586597, 10243739, 11053039, 7473418, 1668476)
+THERE = (16449171, 477046, 13642849, 7670213, 9222927, 4329496, 11130092, 4187066)
+BACK = (12686257, 15687935, 4709462, 3586597, 10243739, 11053032, 7502090, 1639748)
 
 
 def slots_at(places, z):

time: 106 us -> 106 us (level)
  the two profiles are of different devices: /device:TPU:109 before, /device:TPU:103 now
where the time goes in v4:
time: 106 us; the launch traced here: 105 us
  blocking collectives  64.3 us (61%)
  starting transfers between devices  26.7 us (25%)
  waiting for transfers between devices  10.2 us (10%)
  Pallas kernels  3.92 us (4%)
    all_to_all x2, blocking collectives, exchange(): lax.all_to_all(blocks, ('tm', 'space'), 0, 0, axis_index_groups=groups)  64.3 us
    ppermute x2, starting transfers between devices, shards(): across = lax.ppermute(smoothed, axes, far)  22.9 us
    ppermute x2, waiting for transfers between devices, shards(): across = lax.ppermute(smoothed, axes, far)  10.2 us
    ppermute x2, starting transfers between devices, shards(): beside = lax.ppermute(smoothed, axes, near)  3.84 us
  transfers between devices with their start and end apart: 4, of which 2 were waited for; matrix products, arithmetic and copies ran while one was open for 0% of the time, Pallas kernels for 0%

profile of v4, /device:TPU:103, one launch (start us, length us, event | category | flops | bytes accessed | tf_op | source)
XLA Modules:
  0.0 105.2 jit_solution(17097717126733726209)
XLA Ops:
  0.0 1.5 %shard_map.73 = (f32[8,144,128]{2,1,0:T(8,128)S(1)}, f32[4,40,128]{2,1,0:T(8,128)S(1)}) custom-call(f32[4,2,128,128]{3,2,1,0:T(8,128)} %bitcast.12, f32[2,128,128]{2,1,0:T(8,128)} %bitcast.13, f32[2,128,128]{2,1,0:T(8,128)} %bitcast.14, f32[128,128]{1,0:T(8,128)} %bitcast.15, f32[128,128]{1,0:T(8,128)} %bitcast.16, f32[128,128]{1,0:T(8,128)} %bitcast.17, ...), custom_call_target="tpu_custom_call" | custom-call | tf_op jit(solution)/shard_map/pallas_call | solution.py:334
  1.5 28.2 %all_to_all.10.gathered = f32[8,144,128]{2,1,0:T(8,128)S(1)} all-to-all(f32[8,144,128]{2,1,0:T(8,128)S(1)} %get-tuple-element.12), channel_id=1, replica_groups={{320,128,448,0,384,192,64,256},{321,129,449,1,385,193,65,257},{194,258,..., dimensions={0} | all-to-all | bytes 1179648 | tf_op jit(solution)/shard_map/all_to_all | solution.py:51
  29.6 0.5 shard_map.74
  30.1 14.0 %collective-permute-start.1 = (f32[1088,128]{1,0:T(8,128)S(1)}, f32[1088,128]{1,0:T(8,128)S(1)}, u32[]{:S(2)}, u32[]{:S(2)}) collective-permute-start(f32[1088,128]{1,0:T(8,128)S(1)} %get-tuple-element.14), channel_id=1, source_target_pairs={{1,2},{2,1},{3,4},{4,3},{5,6},{6,5},{7,8},{8,7},{9,10},{10,9},{11,... | collective-permute-start | bytes 1671176 | tf_op jit(solution)/shard_map/ppermute | solution.py:339
  44.1 1.9 %collective-permute-start = (f32[1088,128]{1,0:T(8,128)S(1)}, f32[1088,128]{1,0:T(8,128)S(1)}, u32[]{:S(2)}, u32[]{:S(2)}) collective-permute-start(f32[1088,128]{1,0:T(8,128)S(1)} %get-tuple-element.14), channel_id=1, source_target_pairs={{0,1},{1,0},{2,3},{3,2},{4,5},{5,4},{6,7},{7,6},{8,9},{9,8},{10,11... | collective-permute-start | bytes 1671176 | tf_op jit(solution)/shard_map/ppermute | solution.py:340
  46.0 5.3 %collective-permute-done.1.far = f32[1088,128]{1,0:T(8,128)S(1)} collective-permute-done((f32[1088,128]{1,0:T(8,128)S(1)}, f32[1088,128]{1,0:T(8,128)S(1)}, u32[]{:S(2)}, u32[]{:S(2)}) %collective-permute-start.1) | collective-permute-done | bytes 557088 | tf_op jit(solution)/shard_map/ppermute | solution.py:339
  51.3 0.0 collective-permute-done.near
  51.3 0.6 shard_map.75
  51.9 8.9 %collective-permute-start.3 = (f32[1024,128]{1,0:T(8,128)S(1)}, f32[1024,128]{1,0:T(8,128)S(1)}, u32[]{:S(2)}, u32[]{:S(2)}) collective-permute-start(f32[1024,128]{1,0:T(8,128)S(1)} %get-tuple-element.16), channel_id=1, source_target_pairs={{1,2},{2,1},{3,4},{4,3},{5,6},{6,5},{7,8},{8,7},{9,10},{10,9},{11,... | collective-permute-start | bytes 1572872 | tf_op jit(solution)/shard_map/ppermute | solution.py:344
  60.8 1.9 %collective-permute-start.2 = (f32[1024,128]{1,0:T(8,128)S(1)}, f32[1024,128]{1,0:T(8,128)S(1)}, u32[]{:S(2)}, u32[]{:S(2)}) collective-permute-start(f32[1024,128]{1,0:T(8,128)S(1)} %get-tuple-element.16), channel_id=1, source_target_pairs={{0,1},{1,0},{2,3},{3,2},{4,5},{5,4},{6,7},{7,6},{8,9},{9,8},{10,11... | collective-permute-start | bytes 1572872 | tf_op jit(solution)/shard_map/ppermute | solution.py:345
  62.8 4.9 %collective-permute-done.3.far = f32[1024,128]{1,0:T(8,128)S(1)} collective-permute-done((f32[1024,128]{1,0:T(8,128)S(1)}, f32[1024,128]{1,0:T(8,128)S(1)}, u32[]{:S(2)}, u32[]{:S(2)}) %collective-permute-start.3) | collective-permute-done | bytes 524320 | tf_op jit(solution)/shard_map/ppermute | solution.py:344
  67.7 0.0 collective-permute-done.2.near
  67.7 0.5 shard_map.76
  68.2 36.2 %all_to_all.11 = f32[8,128,128]{2,1,0:T(8,128)S(1)} all-to-all(f32[8,128,128]{2,1,0:T(8,128)S(1)} %shard_map.76), channel_id=1, replica_groups={{320,0,384,256,448,192,128,64},{321,1,385,257,449,193,129,65},{450,386,..., dimensions={0} | all-to-all | bytes 1048576 | tf_op jit(solution)/shard_map/all_to_all | solution.py:51
  104.4 0.8 shard_map.77
Async XLA Ops:
  30.1 21.2 %collective-permute-start.1 = (f32[1088,128]{1,0:T(8,128)S(1)}, f32[1088,128]{1,0:T(8,128)S(1)}, u32[]{:S(2)}, u32[]{:S(2)}) collective-permute-start(f32[1088,128]{1,0:T(8,128)S(1)} %get-tuple-element.14), channel_id=1, source_target_pairs={{1,2},{2,1},{3,4},{4,3},{5,6},{6,5},{7,8},{8,7},{9,10},{10,9},{11,... | collective-permute-start | bytes 1671176 | tf_op jit(solution)/shard_map/ppermute | solution.py:339
  44.1 7.2 %collective-permute-start = (f32[1088,128]{1,0:T(8,128)S(1)}, f32[1088,128]{1,0:T(8,128)S(1)}, u32[]{:S(2)}, u32[]{:S(2)}) collective-permute-start(f32[1088,128]{1,0:T(8,128)S(1)} %get-tuple-element.14), channel_id=1, source_target_pairs={{0,1},{1,0},{2,3},{3,2},{4,5},{5,4},{6,7},{7,6},{8,9},{9,8},{10,11... | collective-permute-start | bytes 1671176 | tf_op jit(solution)/shard_map/ppermute | solution.py:340
  51.9 15.7 %collective-permute-start.3 = (f32[1024,128]{1,0:T(8,128)S(1)}, f32[1024,128]{1,0:T(8,128)S(1)}, u32[]{:S(2)}, u32[]{:S(2)}) collective-permute-start(f32[1024,128]{1,0:T(8,128)S(1)} %get-tuple-element.16), channel_id=1, source_target_pairs={{1,2},{2,1},{3,4},{4,3},{5,6},{6,5},{7,8},{8,7},{9,10},{10,9},{11,... | collective-permute-start | bytes 1572872 | tf_op jit(solution)/shard_map/ppermute | solution.py:344
  60.8 6.9 %collective-permute-start.2 = (f32[1024,128]{1,0:T(8,128)S(1)}, f32[1024,128]{1,0:T(8,128)S(1)}, u32[]{:S(2)}, u32[]{:S(2)}) collective-permute-start(f32[1024,128]{1,0:T(8,128)S(1)} %get-tuple-element.16), channel_id=1, source_target_pairs={{0,1},{1,0},{2,3},{3,2},{4,5},{5,4},{6,7},{7,6},{8,9},{9,8},{10,11... | collective-permute-start | bytes 1572872 | tf_op jit(solution)/shard_map/ppermute | solution.py:345

commit v5 on v4

--- a/solution.py
+++ b/solution.py
@@ -139,26 +139,26 @@
     loads = [pltpu.make_async_copy(forcing.at[step], steps.at[step], sems.at[step]) for step in range(4)]
     others = [pltpu.make_async_copy(source, values[i], sems.at[4 + i]) for i, source in enumerate(sources)]
     holds_first = jnp.logical_and(quarter == 0, own_half == 0)
-    for copy in loads + others:
+    for copy in loads[1:] + loads[:1] + others:
         copy.start()
+
+    states = [pltpu.make_async_copy(a, firsts[i], sems.at[8 + i]) for i, a in enumerate((init, prev))]
 
     @pl.when(holds_first)
     def _():
-        pair = [pltpu.make_async_copy(a, firsts[i], sems.at[8 + i]) for i, a in enumerate((init, prev))]
-        for copy in pair:
+        for copy in states:
             copy.start()
-        for copy in pair:
-            copy.wait()
-
-    loads[0].wait()
-
-    @pl.when(holds_first)
-    def _():
-        steps[0] += firsts[0][...] - CORNER * firsts[1][...]
-
-    for step in range(4):
-        if step:
-            loads[step].wait()
+
+    for step in (1, 2, 3, 0):
+        loads[step].wait()
+        if step == 0:
+
+            @pl.when(holds_first)
+            def _():
+                for copy in states:
+                    copy.wait()
+                steps[0] += firsts[0][...] - CORNER * firsts[1][...]
+
         for half in range(2):
             tracer = odd_x if half == 0 else 1 - odd_x
             for part in range(4):

time: 106 us -> 106 us (level)
  no operation moved by 1% of the time
where the time goes in v5:
time: 106 us; the launch traced here: 105 us
  blocking collectives  64.4 us (61%)
  starting transfers between devices  26.7 us (25%)
  waiting for transfers between devices  10.2 us (10%)
  Pallas kernels  3.87 us (4%)
    all_to_all x2, blocking collectives, exchange(): lax.all_to_all(blocks, ('tm', 'space'), 0, 0, axis_index_groups=groups)  64.4 us
    ppermute x2, starting transfers between devices, shards(): across = lax.ppermute(smoothed, axes, far)  22.9 us
    ppermute x2, waiting for transfers between devices, shards(): across = lax.ppermute(smoothed, axes, far)  10.2 us
    ppermute x2, starting transfers between devices, shards(): beside = lax.ppermute(smoothed, axes, near)  3.84 us
  transfers between devices with their start and end apart: 4, of which 2 were waited for; matrix products, arithmetic and copies ran while one was open for 0% of the time, Pallas kernels for 0%

profile of v5, /device:TPU:103, one launch (start us, length us, event | category | flops | bytes accessed | tf_op | source)
XLA Modules:
  0.0 105.2 jit_solution(3816319516737708574)
XLA Ops:
  0.0 1.4 %shard_map.73 = (f32[8,144,128]{2,1,0:T(8,128)S(1)}, f32[4,40,128]{2,1,0:T(8,128)S(1)}) custom-call(f32[4,2,128,128]{3,2,1,0:T(8,128)} %bitcast.12, f32[2,128,128]{2,1,0:T(8,128)} %bitcast.13, f32[2,128,128]{2,1,0:T(8,128)} %bitcast.14, f32[128,128]{1,0:T(8,128)} %bitcast.15, f32[128,128]{1,0:T(8,128)} %bitcast.16, f32[128,128]{1,0:T(8,128)} %bitcast.17, ...), custom_call_target="tpu_custom_call" | custom-call | tf_op jit(solution)/shard_map/pallas_call | solution.py:334
  1.4 28.2 %all_to_all.10.gathered = f32[8,144,128]{2,1,0:T(8,128)S(1)} all-to-all(f32[8,144,128]{2,1,0:T(8,128)S(1)} %get-tuple-element.12), channel_id=1, replica_groups={{320,128,448,0,384,192,64,256},{321,129,449,1,385,193,65,257},{194,258,..., dimensions={0} | all-to-all | bytes 1179648 | tf_op jit(solution)/shard_map/all_to_all | solution.py:51
  29.6 0.5 shard_map.74
  30.1 14.0 %collective-permute-start.1 = (f32[1088,128]{1,0:T(8,128)S(1)}, f32[1088,128]{1,0:T(8,128)S(1)}, u32[]{:S(2)}, u32[]{:S(2)}) collective-permute-start(f32[1088,128]{1,0:T(8,128)S(1)} %get-tuple-element.14), channel_id=1, source_target_pairs={{1,2},{2,1},{3,4},{4,3},{5,6},{6,5},{7,8},{8,7},{9,10},{10,9},{11,... | collective-permute-start | bytes 1671176 | tf_op jit(solution)/shard_map/ppermute | solution.py:339
  44.1 1.9 %collective-permute-start = (f32[1088,128]{1,0:T(8,128)S(1)}, f32[1088,128]{1,0:T(8,128)S(1)}, u32[]{:S(2)}, u32[]{:S(2)}) collective-permute-start(f32[1088,128]{1,0:T(8,128)S(1)} %get-tuple-element.14), channel_id=1, source_target_pairs={{0,1},{1,0},{2,3},{3,2},{4,5},{5,4},{6,7},{7,6},{8,9},{9,8},{10,11... | collective-permute-start | bytes 1671176 | tf_op jit(solution)/shard_map/ppermute | solution.py:340
  46.0 5.3 %collective-permute-done.1.far = f32[1088,128]{1,0:T(8,128)S(1)} collective-permute-done((f32[1088,128]{1,0:T(8,128)S(1)}, f32[1088,128]{1,0:T(8,128)S(1)}, u32[]{:S(2)}, u32[]{:S(2)}) %collective-permute-start.1) | collective-permute-done | bytes 557088 | tf_op jit(solution)/shard_map/ppermute | solution.py:339
  51.3 0.0 collective-permute-done.near
  51.3 0.6 shard_map.75
  51.9 8.9 %collective-permute-start.3 = (f32[1024,128]{1,0:T(8,128)S(1)}, f32[1024,128]{1,0:T(8,128)S(1)}, u32[]{:S(2)}, u32[]{:S(2)}) collective-permute-start(f32[1024,128]{1,0:T(8,128)S(1)} %get-tuple-element.16), channel_id=1, source_target_pairs={{1,2},{2,1},{3,4},{4,3},{5,6},{6,5},{7,8},{8,7},{9,10},{10,9},{11,... | collective-permute-start | bytes 1572872 | tf_op jit(solution)/shard_map/ppermute | solution.py:344
  60.8 1.9 %collective-permute-start.2 = (f32[1024,128]{1,0:T(8,128)S(1)}, f32[1024,128]{1,0:T(8,128)S(1)}, u32[]{:S(2)}, u32[]{:S(2)}) collective-permute-start(f32[1024,128]{1,0:T(8,128)S(1)} %get-tuple-element.16), channel_id=1, source_target_pairs={{0,1},{1,0},{2,3},{3,2},{4,5},{5,4},{6,7},{7,6},{8,9},{9,8},{10,11... | collective-permute-start | bytes 1572872 | tf_op jit(solution)/shard_map/ppermute | solution.py:345
  62.8 4.9 %collective-permute-done.3.far = f32[1024,128]{1,0:T(8,128)S(1)} collective-permute-done((f32[1024,128]{1,0:T(8,128)S(1)}, f32[1024,128]{1,0:T(8,128)S(1)}, u32[]{:S(2)}, u32[]{:S(2)}) %collective-permute-start.3) | collective-permute-done | bytes 524320 | tf_op jit(solution)/shard_map/ppermute | solution.py:344
  67.7 0.0 collective-permute-done.2.near
  67.7 0.5 shard_map.76
  68.2 36.2 %all_to_all.11 = f32[8,128,128]{2,1,0:T(8,128)S(1)} all-to-all(f32[8,128,128]{2,1,0:T(8,128)S(1)} %shard_map.76), channel_id=1, replica_groups={{320,0,384,256,448,192,128,64},{321,1,385,257,449,193,129,65},{450,386,..., dimensions={0} | all-to-all | bytes 1048576 | tf_op jit(solution)/shard_map/all_to_all | solution.py:51
  104.4 0.8 shard_map.77
Async XLA Ops:
  30.1 21.2 %collective-permute-start.1 = (f32[1088,128]{1,0:T(8,128)S(1)}, f32[1088,128]{1,0:T(8,128)S(1)}, u32[]{:S(2)}, u32[]{:S(2)}) collective-permute-start(f32[1088,128]{1,0:T(8,128)S(1)} %get-tuple-element.14), channel_id=1, source_target_pairs={{1,2},{2,1},{3,4},{4,3},{5,6},{6,5},{7,8},{8,7},{9,10},{10,9},{11,... | collective-permute-start | bytes 1671176 | tf_op jit(solution)/shard_map/ppermute | solution.py:339
  44.1 7.2 %collective-permute-start = (f32[1088,128]{1,0:T(8,128)S(1)}, f32[1088,128]{1,0:T(8,128)S(1)}, u32[]{:S(2)}, u32[]{:S(2)}) collective-permute-start(f32[1088,128]{1,0:T(8,128)S(1)} %get-tuple-element.14), channel_id=1, source_target_pairs={{0,1},{1,0},{2,3},{3,2},{4,5},{5,4},{6,7},{7,6},{8,9},{9,8},{10,11... | collective-permute-start | bytes 1671176 | tf_op jit(solution)/shard_map/ppermute | solution.py:340
  51.9 15.7 %collective-permute-start.3 = (f32[1024,128]{1,0:T(8,128)S(1)}, f32[1024,128]{1,0:T(8,128)S(1)}, u32[]{:S(2)}, u32[]{:S(2)}) collective-permute-start(f32[1024,128]{1,0:T(8,128)S(1)} %get-tuple-element.16), channel_id=1, source_target_pairs={{1,2},{2,1},{3,4},{4,3},{5,6},{6,5},{7,8},{8,7},{9,10},{10,9},{11,... | collective-permute-start | bytes 1572872 | tf_op jit(solution)/shard_map/ppermute | solution.py:344
  60.8 6.9 %collective-permute-start.2 = (f32[1024,128]{1,0:T(8,128)S(1)}, f32[1024,128]{1,0:T(8,128)S(1)}, u32[]{:S(2)}, u32[]{:S(2)}) collective-permute-start(f32[1024,128]{1,0:T(8,128)S(1)} %get-tuple-element.16), channel_id=1, source_target_pairs={{0,1},{1,0},{2,3},{3,2},{4,5},{5,4},{6,7},{7,6},{8,9},{9,8},{10,11... | collective-permute-start | bytes 1572872 | tf_op jit(solution)/shard_map/ppermute | solution.py:345
